TPU v7x, 512 devices: a whole 4x8x8 slice. The times are simulated.
512 devices in a mesh: rel: 8 (over y), dom: 64 (over z, x, core).
Axes of the slice: x: 4, y: 8, z: 8, core: 2. Of those that a mesh axis runs over, the one named last changes fastest.
Arguments:
- node_feats: bfloat16 [16384, 1024], P('dom'), may hold values from -6 to 6
- rel_weight: bfloat16 [8, 1024, 1024], P('rel'), may hold values from -0.1875 to 0.1875
- att_src: float32 [8, 1024], P('rel')
- att_dst: float32 [8, 1024], P('rel')
- src_row: int32 [8, 64, 64, 16], P('rel', 'dom'), may hold values from 0 to 255, as said below
- dst_row: int32 [8, 64, 64, 16], P('rel', 'dom'), may hold values from -1 to 255, as said below
Outputs:
- aggregated: bfloat16 [16384, 1024], P('dom', 'rel')
Inputs may be any that keep to these rules, and one draw needn't show every extreme that they name: Slot k of the pair (p, q) describes the same edge in src_row[r, p, q, k] and dst_row[r, q, p, k]. Each pair's live slots come first; each pair has 1 to 16 edges, and in every relation some target partition receives 16 edges from every source partition. Source rows of empty slots are arbitrary valid rows. `dst_row`: -1 marks an empty slot.
All inputs are finite; a program needn't handle non-finite values.
Results may differ from a plain program's by a relative error of at most 0.015.
Values may be sent and summed in bfloat16 or wider, within the bound.
A program may use at most 64 MiB of HBM per device.

v0:
```python
import jax
import jax.numpy as jnp
from jax import lax
from jax.sharding import PartitionSpec as P

HEADS = 4


def head_matrix(vector):
    width = vector.shape[0]
    mask = (jnp.arange(width) // (width // HEADS))[:, None] == jnp.arange(HEADS)[None, :]
    return jnp.where(mask, vector[:, None], jnp.zeros((), jnp.float32))


def on_device(node_feats, rel_weight, att_src, att_dst, src_row, dst_row):
    weight = rel_weight[0]
    node_rows = node_feats.shape[0]
    feat_width = node_feats.shape[1]
    peer_count = lax.axis_size("dom")
    slot_cap = src_row.shape[3]
    slot_total = peer_count * slot_cap
    src_pick = src_row.reshape(slot_total)
    own_proj = jnp.dot(node_feats, weight, preferred_element_type=jnp.float32).astype(jnp.bfloat16)
    outgoing = own_proj[src_pick].reshape(peer_count, slot_cap, feat_width)
    arrived = lax.all_to_all(outgoing, "dom", split_axis=0, concat_axis=0, tiled=True)
    edge_proj = arrived.reshape(slot_total, feat_width)
    src_score = jnp.dot(
        edge_proj.astype(jnp.float32), head_matrix(att_src[0]), precision=lax.Precision.HIGHEST
    )
    dst_score = jnp.dot(
        own_proj.astype(jnp.float32), head_matrix(att_dst[0]), precision=lax.Precision.HIGHEST
    )
    target = dst_row.reshape(slot_total)
    is_valid = target >= 0
    segment = jnp.where(is_valid, target, node_rows)
    score = jax.nn.leaky_relu(src_score + dst_score[jnp.minimum(segment, node_rows - 1)], 0.2)
    score = jnp.where(is_valid[:, None], score, jnp.float32(-1e30))
    peak_score = jax.ops.segment_max(score, segment, node_rows + 1)
    expo = jnp.where(is_valid[:, None], jnp.exp(score - peak_score[segment]), jnp.float32(0.0))
    seg_total = jax.ops.segment_sum(expo, segment, node_rows + 1)
    attn_weight = expo / jnp.where(is_valid[:, None], seg_total[segment], jnp.float32(1.0))
    message = (
        (
            edge_proj.reshape(slot_total, HEADS, feat_width // HEADS).astype(jnp.float32)
            * attn_weight[:, :, None]
        )
        .reshape(slot_total, feat_width)
        .astype(jnp.bfloat16)
    )
    onehot = (segment[None, :] == jnp.arange(node_rows)[:, None]).astype(jnp.bfloat16)
    partial_value = jnp.dot(onehot, message, preferred_element_type=jnp.float32)
    combined = lax.psum_scatter(
        partial_value.astype(jnp.bfloat16), "rel", scatter_dimension=1, tiled=True
    )
    return combined


def solution(mesh):
    placed = (
        P("dom", None),
        P("rel", None, None),
        P("rel", None),
        P("rel", None),
        P("rel", "dom", None, None),
        P("rel", "dom", None, None),
    )
    return jax.shard_map(
        on_device, mesh=mesh, in_specs=placed, out_specs=P("dom", "rel"), check_vma=False
    )
```

profile of v0, /device:TPU:6, one launch (start us, length us, event | category | flops | bytes accessed | tf_op | source)
XLA Modules:
  0.0 152.9 jit_solution(14640027080682071267)
XLA Ops:
  6.5 0.0 copy-start
  6.5 0.9 copy.23
  7.5 0.1 reshape.126
  7.6 0.6 copy-done
  8.1 1.7 %fusion.4 = bf16[256,1024]{1,0:T(8,128)(2,1)S(1)} fusion(bf16[256,1024]{1,0:T(8,128)(2,1)} %param.6, bf16[1,1024,1024]{2,1,0:T(8,128)(2,1)S(1)} %copy-done), kind=kOutput, calls=%fused_computation.11 | convolution fusion | flops 537133056 | bytes 3145728 | tf_op jit(solution)/shard_map/dot_general | solution.py:23
  9.9 5.4 %gather_fusion = bf16[1024,1024]{1,0:T(8,128)(2,1)} fusion(bf16[256,1024]{1,0:T(8,128)(2,1)S(1)} %fusion.4, s32[1024]{0:T(1024)S(1)} %broadcast_clamp_fusion.2), kind=kCustom, calls=%fused_computation | custom fusion | bytes 4198400 | tf_op jit(solution)/shard_map/gather | solution.py:24
  15.3 0.0 copy-start.1
  15.3 0.0 copy-start.3
  15.3 14.1 %all-to-all-start = ((bf16[64,16,1024]{2,1,0:T(8,128)(2,1)}), bf16[64,16,1024]{2,1,0:T(8,128)(2,1)}, u32[]{:S(2)}, u32[]{:S(2)}) async-start(bf16[64,16,1024]{2,1,0:T(8,128)(2,1)} %bitcast.28), calls=%async_computation | async-start | bytes 4194304 | tf_op jit(solution)/shard_map/all_to_all | solution.py:25
  29.4 0.0 reduce-scatter.4.cloned.1.call-start
  29.5 0.0 copy-done.1
  29.5 0.1 copy.22
  29.6 0.1 reshape.125
  29.7 0.1 reshape.128
  29.8 0.0 copy-done.3
  29.8 0.6 fusion.13
  30.4 0.0 copy-start.2
  30.4 2.8 %gather_fusion.1 = f32[1024,4]{1,0:T(8,128)S(1)} fusion(f32[256,4]{1,0:T(8,128)S(1)} %fusion.13, s32[1024]{0:T(1024)S(1)} %broadcast_clamp_fusion.1), kind=kCustom, calls=%fused_computation.1 | custom fusion | bytes 36864 | tf_op jit(solution)/shard_map/gather | solution.py:36
  33.2 0.2 copy.26
  33.4 47.2 %all-to-all-done = bf16[64,16,1024]{2,1,0:T(8,128)(2,1)} async-done(((bf16[64,16,1024]{2,1,0:T(8,128)(2,1)}), bf16[64,16,1024]{2,1,0:T(8,128)(2,1)}, u32[]{:S(2)}, u32[]{:S(2)}) %all-to-all-start) | async-done | bytes 2097184 | tf_op jit(solution)/shard_map/all_to_all | solution.py:25
  80.6 0.0 copy-done.2
  80.6 3.3 %fusion.12 = f32[1024,4]{0,1:T(4,128)S(1)} fusion(f32[1024,4]{0,1:T(4,128)S(1)} %copy.26, bf16[1024,1024]{1,0:T(8,128)(2,1)} %bitcast.3, f32[1024]{0:T(1024)S(1)} %bitcast.34, s32[1024]{0:T(1024)S(1)} %add_select_fusion, pred[1024]{0:T(1024)(128)(4,1)S(1)} %broadcast_compare_fusion), kind=kOutput, calls=%fused_computation.20 | convolution fusion | flops 50360320 | bytes 2139136 | tf_op jit(solution)/shard_map/dot_general | solution.py:27
  84.0 0.2 copy.27
  84.2 6.1 %scatter_custom_fusion = f32[257,4]{1,0:T(8,128)S(1)} fusion(s32[1024]{0:T(1024)S(1)} %bitcast.35, f32[1024,4]{1,0:T(8,128)S(1)} %copy.27, f32[]{:T(128)} %constant.36.clone.1), kind=kCustom, calls=%fused_computation.17 | custom fusion | flops 4096 | bytes 4116 | tf_op jit(solution)/shard_map/scatter-max | solution.py:38
  90.3 2.8 %gather_fusion.2 = f32[1024,4]{1,0:T(8,128)S(1)} fusion(f32[257,4]{1,0:T(8,128)S(1)} %scatter_custom_fusion, s32[1024]{0:T(1024)S(1)} %broadcast_clamp_fusion), kind=kCustom, calls=%fused_computation.2 | custom fusion | bytes 36864 | tf_op jit(solution)/shard_map/gather | solution.py:39
  93.1 0.2 copy.28
  93.3 0.2 copy.29
  93.6 6.1 %scatter_custom_fusion.1 = f32[257,4]{1,0:T(8,128)S(1)} fusion(s32[1024]{0:T(1024)S(1)} %bitcast.36, f32[1024,4]{1,0:T(8,128)S(1)} %copy.29, f32[]{:T(128)} %constant.33.clone.1), kind=kCustom, calls=%fused_computation.15 | custom fusion | flops 4096 | bytes 4116 | tf_op jit(solution)/shard_map/scatter-add | solution.py:40
  99.6 2.8 %gather_fusion.3 = f32[1024,4]{1,0:T(8,128)S(1)} fusion(f32[257,4]{1,0:T(8,128)S(1)} %scatter_custom_fusion.1, s32[1024]{0:T(1024)S(1)} %broadcast_clamp_fusion), kind=kCustom, calls=%fused_computation.3 | custom fusion | bytes 36864 | tf_op jit(solution)/shard_map/gather | solution.py:41
  102.5 0.2 copy.30
  102.7 0.2 copy.31
  102.9 1.2 mul.21
  104.2 1.0 copy.35
  105.2 2.4 %fusion.3 = bf16[256,1024]{1,0:T(8,128)(2,1)S(1)} fusion(f32[1024,1024]{1,0:T(8,128)S(1)} %bitcast.26, bf16[1024,1024]{1,0:T(8,128)(2,1)} %bitcast.3, s32[1024]{0:T(1024)S(1)} %broadcast_select_fusion), kind=kOutput, calls=%fused_computation.10 | convolution fusion | flops 540540928 | bytes 6819840 | tf_op jit(solution)/shard_map/dot_general | solution.py:51
  107.6 1.0 copy.33
  108.5 0.0 reduce-scatter.4.cloned.1.call-update
  108.6 35.9 %reduce-scatter.4.cloned.1.call-done = bf16[128,256]{1,0:T(8,128)(2,1)} async-done(((bf16[1024,256]{1,0:T(8,128)(2,1)}), bf16[128,256]{1,0:T(8,128)(2,1)}) %reduce-scatter.4.cloned.1.call-update) | async-done | bytes 65552
  144.5 1.6 %copy.34 = bf16[256,128]{1,0:T(8,128)(2,1)} copy(bf16[256,128]{0,1:T(8,128)(2,1)} %bitcast.30) | data formatting | bytes 131072
  (10 shorter events, 0.1 us)
Async XLA Ops:
  6.5 1.6 %copy-start = (bf16[1,1024,1024]{2,1,0:T(8,128)(2,1)S(1)}, bf16[1,1024,1024]{2,1,0:T(8,128)(2,1)}, u32[]{:S(2)}) copy-start(bf16[1,1024,1024]{2,1,0:T(8,128)(2,1)} %param.7) | copy-start | bytes 6291460
  15.3 14.2 %copy-start.1 = (s32[1,1,64,16]{2,3,1,0:T(8,128)S(1)}, s32[1,1,64,16]{2,3,1,0:T(8,128)}, u32[]{:S(2)}) copy-start(s32[1,1,64,16]{2,3,1,0:T(8,128)} %param.11) | copy-start | bytes 12292
  15.3 14.5 %copy-start.3 = (f32[1,1024]{1,0:T(1,128)S(1)}, f32[1,1024]{1,0:T(1,128)}, u32[]{:S(2)}) copy-start(f32[1,1024]{1,0:T(1,128)} %param.9) | copy-start | bytes 12292
  15.3 65.3 %all-to-all-start = ((bf16[64,16,1024]{2,1,0:T(8,128)(2,1)}), bf16[64,16,1024]{2,1,0:T(8,128)(2,1)}, u32[]{:S(2)}, u32[]{:S(2)}) async-start(bf16[64,16,1024]{2,1,0:T(8,128)(2,1)} %bitcast.28), calls=%async_computation | async-start | bytes 4194304 | tf_op jit(solution)/shard_map/all_to_all | solution.py:25
  29.4 115.0 %reduce-scatter.4.cloned.1.call-start = ((), (), s32[]{:S(2)}) async-start(), calls=%async_computation.2 | async-start | bytes 589824
  30.4 50.3 %copy-start.2 = (f32[1,1024]{1,0:T(1,128)S(1)}, f32[1,1024]{1,0:T(1,128)}, u32[]{:S(2)}) copy-start(f32[1,1024]{1,0:T(1,128)} %param.8) | copy-start | bytes 12292
Sparse Core Ops, SparseCore 0:
  108.7 35.7 reduce-scatter.3
where the time goes:
time: 153 us
  waiting for transfers between devices  83.2 us (54%)
  local copies, waits for them, and re-layouts  21.7 us (14%)
  starting transfers between devices  14.2 us (9%)
  between operations  13.6 us (9%)
  other arithmetic  12.3 us (8%)
  matrix products  8 us (5%)
    all_to_all x1, waiting for transfers between devices, on_device(): lax.all_to_all(outgoing, 'dom', split_axis=0, concat_axis=0, tiled=True)  47.2 us
    unnamed x2, waiting for transfers between devices  35.9 us
    all_to_all x1, starting transfers between devices, on_device(): lax.all_to_all(outgoing, 'dom', split_axis=0, concat_axis=0, tiled=True)  14.1 us
    another operation x1, other arithmetic, on_device(): peak_score = jax.ops.segment_max(score, segment, node_rows + 1)  6.08 us
    scatter-add x1, other arithmetic, on_device(): seg_total = jax.ops.segment_sum(expo, segment, node_rows + 1)  6.08 us
    gather x1, local copies, waits for them, and re-layouts, on_device(): outgoing = own_proj[src_pick].reshape(peer_count, slot_cap, feat_width)  5.39 us
    unnamed x13, local copies, waits for them, and re-layouts  5.16 us
    dot_general x1, matrix products, on_device(): jnp.dot(edge_proj.astype(jnp.float32), head_matrix(att_src[0]), precision...  3.31 us
  transfers between devices with their start and end apart: 2, of which 2 were waited for; matrix products, arithmetic and copies ran while one was open for 3% of the time, Pallas kernels for 0%

commit v1 on v0

v1 whole, which is shorter than its diff:
```python
import jax
import jax.numpy as jnp
from jax import lax
from jax.experimental import pallas as pl
from jax.experimental.pallas import tpu as pltpu
from jax.sharding import PartitionSpec as P

MESH = pl.DeviceIdType.MESH
HEADS = 4
N = 256
D = 1024
CB = 128
G = 8
ZN = 8
RN = 8
F32 = jnp.float32
BF = jnp.bfloat16
ORDER = (0, 1, 7, 2, 6, 3, 5, 4)
TO_RIGHT = (0, 7, 2, 5)


def split3(v):
    hi = v.astype(BF).astype(F32)
    rest = v - hi
    mid = rest.astype(BF).astype(F32)
    low = rest - mid
    return jnp.concatenate([hi, mid, low, jnp.zeros_like(v)], axis=0).astype(BF)


def join3(v):
    return v[0:8] + v[8:16] + v[16:24]


def leaky(v):
    return jnp.where(v >= 0, v, 0.2 * v)


def dot(a, b):
    return jnp.dot(a, b, preferred_element_type=F32)


def dot_nt(a, b):
    return lax.dot_general(a, b, (((1,), (1,)), ((), ())), preferred_element_type=F32)


def block_transpose(tiles):
    lane_block = lax.broadcasted_iota(jnp.int32, (8, 128), 1) // 16
    for bit in (1, 2, 4):
        low = (lane_block & bit) == 0
        out = list(tiles)
        for i in range(8):
            if i & bit:
                continue
            first, second = tiles[i], tiles[i + bit]
            out[i] = jnp.where(low, first, pltpu.roll(second, 16 * bit, 1))
            out[i + bit] = jnp.where(low, pltpu.roll(first, 128 - 16 * bit, 1), second)
        tiles = out
    return tiles


def kernel(
    feat_ref, w_ref, asrc_ref, adst_ref, src_ref, dst_ref, out_ref,
    x_buf, w_buf, proj, pall, onehot, picked,
    idx_send, idx_recv, idx_rows, idx_all,
    s1, r1, s2, r2, s3, r3, al_send, al_all,
    max_cols, dst_hot, expo,
    zs_r, zs_l, zr_r, zr_l,
    in_sem, y_ss, y_rs, x_ss, x_rs, g_ss, g_rs, h_ss, h_rs, k_ss, k_rs, m_ss, m_rs, n_ss, n_rs, o_ss, o_rs, z_ss, z_rs,
):
    r = lax.axis_index("rel")
    p = lax.axis_index("dom")
    z, g = p // G, p % G
    x, a = g // 2, g % 2
    load_x = pltpu.make_async_copy(feat_ref, x_buf, in_sem.at[0])
    load_w = pltpu.make_async_copy(w_ref, w_buf, in_sem.at[1])
    load_x.start()
    load_w.start()

    def in_group(i):
        return (r, z * G + i)

    def in_z(i):
        return (r, i * G + g)

    def in_rel(i):
        return (i, p)

    def hop(i, amount, size):
        return lax.rem(i + amount + size, size)

    barrier = pltpu.get_barrier_semaphore()
    for d in range(1, 8):
        for dev in (in_group(hop(g, d, G)), in_z(hop(z, d, ZN)), in_rel(hop(r, d, RN))):
            pl.semaphore_signal(barrier, inc=1, device_id=dev, device_id_type=MESH)
    pl.semaphore_wait(barrier, 21)

    sent = []

    def copy(src, dst, ss, rs, dev):
        return pltpu.make_async_remote_copy(
            src_ref=src, dst_ref=dst, send_sem=ss, recv_sem=rs, device_id=dev, device_id_type=MESH
        )

    def send(*args):
        c = copy(*args)
        c.start()
        sent.append(c)

    def exchange(sbuf, rbuf, ss, rs, me, member):
        rbuf[me] = sbuf[me]
        for d in range(1, 8):
            to = hop(me, d, 8)
            send(sbuf.at[to], rbuf.at[me], ss.at[d], rs.at[8 - d], member(to))

    def arrived(sbuf, rbuf, ss, rs, me, member):
        for d in range(1, 8):
            frm = hop(me, d, 8)
            copy(sbuf.at[frm], rbuf.at[frm], ss.at[d], rs.at[d], member(frm)).wait_recv()

    src_f = src_ref[...].astype(F32)
    for i in range(G):
        idx_send[i] = jnp.broadcast_to(src_f[i : i + 1], (8, 128))
    exchange(idx_send, idx_recv, g_ss, g_rs, g, in_group)

    load_x.wait()
    load_w.wait()
    feats = x_buf[...]
    for i in range(4):
        part = dot(feats, w_buf[:, 256 * i : 256 * (i + 1)]).astype(BF)
        proj[2 * i] = part[:, :CB]
        proj[2 * i + 1] = part[:, CB:]

    arrived(idx_send, idx_recv, g_ss, g_rs, g, in_group)
    for i in range(G):
        idx_rows[i : i + 1, :] = idx_recv[i, 0:1, :]
    idx_all[0] = idx_rows[...]
    for d in range(1, 8):
        send(idx_rows, idx_all.at[8 - d], h_ss.at[d], h_rs.at[8 - d], in_rel(hop(r, d, RN)))

    pall[g, 0] = proj[r]
    for d in ORDER[1:]:
        to = hop(r, d, RN)
        send(proj.at[to], pall.at[g, 8 - d], y_ss.at[d], y_rs.at[8 - d], in_rel(to))

    x_r, x_l, x_2 = hop(x, 1, 4), hop(x, 3, 4), hop(x, 2, 4)
    g_r, g_l, g_2 = 2 * x_r + a, 2 * x_l + a, 2 * x_2 + a
    partner = 2 * x + 1 - a

    def give(kind, j, owner, to):
        send(pall.at[owner, j], pall.at[owner, j], x_ss.at[kind, j], x_rs.at[kind, j], in_group(to))

    def got(kind, j, owner):
        copy(pall.at[owner, j], pall.at[owner, j], x_ss.at[kind, j], x_rs.at[kind, j], in_group(partner)).wait_recv()

    def stage_own(j):
        if j:
            copy(proj.at[0], pall.at[g, j], y_ss.at[j], y_rs.at[j], in_rel(hop(r, j, RN))).wait_recv()
        give(0, j, g, g_r)
        give(1, j, g, g_l)
        give(3, j, g, partner)

    def stage_near(j):
        got(0, j, g_l)
        if j in TO_RIGHT:
            give(2, j, g_l, g_r)
        give(4, j, g_l, partner)
        got(1, j, g_r)
        if j not in TO_RIGHT:
            give(2, j, g_r, g_l)
        give(5, j, g_r, partner)

    def stage_far(j):
        got(2, j, g_2)
        give(6, j, g_2, partner)

    def stage_pick(j):
        got(3, j, partner)
        got(4, j, 2 * x_l + 1 - a)
        got(5, j, 2 * x_r + 1 - a)
        got(6, j, 2 * x_2 + 1 - a)

        def body(i, carry):
            rows = dot(onehot[j, i], pall[i, j]).astype(BF)
            picked[:, pl.ds(pl.multiple_of(j * 128 + i * 16, 16), 16), :] = rows.reshape(ZN, 16, CB)
            return carry

        lax.fori_loop(0, G, body, 0)

    stage_own(0)

    row8 = lax.broadcasted_iota(jnp.int32, (8, D), 0)
    lane8 = lax.broadcasted_iota(jnp.int32, (8, D), 1)
    att = jnp.where(row8 < HEADS, asrc_ref[...], adst_ref[...])
    att = split3(jnp.where(lane8 // (D // HEADS) == row8 % HEADS, att, 0.0))
    total = jnp.zeros((32, N), F32)
    for c in range(RN):
        total = total + dot_nt(att[:, CB * c : CB * (c + 1)], proj[c])
    score = join3(total)
    score3 = split3(score)

    iota_n = lax.broadcasted_iota(jnp.int32, (N, 128), 0)
    src_i = src_ref[...]
    for i in range(G):
        hot = jnp.where(src_i[i : i + 1] == iota_n, 1.0, 0.0).astype(BF)
        s1[i] = join3(dot(score3, hot))
    exchange(s1, r1, k_ss, k_rs, g, in_group)

    stage_own(1)

    arrived(s1, r1, k_ss, k_rs, g, in_group)
    for i, tile in enumerate(block_transpose([r1[i] for i in range(G)])):
        s2[i] = tile
    exchange(s2, r2, m_ss, m_rs, z, in_z)

    stage_own(7)
    stage_near(0)

    for d in range(1, 8):
        copy(idx_rows, idx_all.at[d], h_ss.at[d], h_rs.at[d], in_rel(hop(r, d, RN))).wait_recv()
    iota_l = lax.broadcasted_iota(jnp.int32, (128, N), 1).astype(F32)

    def hot_body(j, carry):
        cols = idx_all[j].T
        for i in range(G):
            onehot[j, i] = jnp.where(cols[:, i : i + 1] == iota_l, 1.0, 0.0).astype(BF)
        return carry

    lax.fori_loop(0, RN, hot_body, 0)

    arrived(s2, r2, m_ss, m_rs, z, in_z)
    row = lax.broadcasted_iota(jnp.int32, (8, 128), 0)
    lane = lax.broadcasted_iota(jnp.int32, (64, 128), 1)
    neg = -jnp.inf

    def max_body(t, carry):
        base = pl.multiple_of(t * 64, 64)
        iota_t = lax.broadcasted_iota(jnp.int32, (64, 128), 0) + base
        best = [jnp.full((64, 128), neg, F32) for _ in range(HEADS)]
        for i in range(ZN):
            mask = dst_ref[i : i + 1, :] == iota_t
            dst_hot[i, pl.ds(base, 64), :] = jnp.where(mask, 1.0, 0.0).astype(BF)
            for h in range(HEADS):
                best[h] = jnp.maximum(best[h], jnp.where(mask, r2[i, h : h + 1, :], neg))
        cols = jnp.zeros((64, 128), F32)
        for h in range(HEADS):
            cols = jnp.where(lane == h, jnp.max(best[h], axis=1, keepdims=True), cols)
        max_cols[pl.ds(base, 64), :] = cols
        return carry

    lax.fori_loop(0, 4, max_body, 0)
    peak_src = max_cols[...].T[0:8]
    row_n = lax.broadcasted_iota(jnp.int32, (8, N), 0)
    dst_up = pltpu.roll(score, 4, 0)
    peak = jnp.where(peak_src == neg, 0.0, leaky(peak_src + dst_up))
    table = split3(jnp.where(row_n < HEADS, peak, score))
    seg = jnp.zeros((32, N), F32)
    for i in range(ZN):
        near = join3(dot(table, dst_hot[i]))
        edge = leaky(r2[i] + pltpu.roll(near, 4, 0))
        live = (row < HEADS) & (dst_ref[i : i + 1, :] >= 0)
        e = jnp.where(live, jnp.exp(jnp.where(live, edge - near, 0.0)), 0.0)
        expo[i] = e
        seg = seg + dot_nt(split3(e), dst_hot[i])
    seg3 = split3(join3(seg))
    for i in range(ZN):
        live = (row < HEADS) & (dst_ref[i : i + 1, :] >= 0)
        under = jnp.where(live, join3(dot(seg3, dst_hot[i])), 1.0)
        alpha = jnp.where(live, expo[i] / under, 0.0)
        s3[i] = jnp.where(row == HEADS, dst_ref[i : i + 1, :].astype(F32), alpha)
    exchange(s3, r3, n_ss, n_rs, z, in_z)

    stage_own(2)
    stage_near(1)
    stage_own(6)

    arrived(s3, r3, n_ss, n_rs, z, in_z)
    for h in range(HEADS):
        al_send[h, 0:8] = r3[:, h, :]
        al_send[h, 8:16] = r3[:, HEADS, :]
    al_all[0] = al_send[r // 2]
    for d in range(1, 8):
        to = hop(r, d, RN)
        send(al_send.at[to // 2], al_all.at[8 - d], o_ss.at[d], o_rs.at[8 - d], in_rel(to))

    stage_near(7)
    stage_far(0)
    stage_own(3)
    stage_near(2)
    stage_far(1)
    stage_own(5)
    stage_pick(0)
    stage_near(6)
    stage_far(7)
    stage_own(4)
    stage_pick(1)
    stage_near(3)
    stage_far(2)
    stage_pick(7)
    stage_near(5)
    stage_far(6)
    stage_pick(2)
    stage_near(4)
    stage_far(3)
    stage_pick(6)
    stage_far(5)
    stage_pick(3)
    stage_far(4)
    stage_pick(5)
    stage_pick(4)

    for d in range(1, 8):
        copy(al_send.at[0], al_all.at[d], o_ss.at[d], o_rs.at[d], in_rel(hop(r, d, RN))).wait_recv()

    def part(zt):
        acc = jnp.zeros((N, CB), F32)
        for j in range(0, RN, 2):
            both = []
            for jj in (j, j + 1):
                alpha = al_all[jj, pl.ds(zt, 1), :]
                target = al_all[jj, pl.ds(zt + 8, 1), :]
                both.append(jnp.where(target == iota_n.astype(F32), alpha, 0.0).astype(BF))
            acc = acc + dot(jnp.concatenate(both, axis=1), picked[zt, j * 128 : j * 128 + 256, :])
        return acc

    right, left = in_z(hop(z, 1, ZN)), in_z(hop(z, -1, ZN))
    half = N // 2

    def ring(way, s, dev):
        sbuf, rbuf = (zs_r, zr_r) if way == 0 else (zs_l, zr_l)
        rows = pl.ds(half * way, half) if s == 0 else pl.ds(0, N)
        return copy(sbuf.at[s, rows], rbuf.at[s, rows], z_ss.at[way, s], z_rs.at[way, s], dev)

    def ring_send(way, s, dev):
        c = ring(way, s, dev)
        c.start()
        sent.append(c)

    far = part(hop(z, 4, ZN)).astype(BF)
    zs_r[0, 0:half] = far[0:half]
    ring_send(0, 0, right)
    zs_l[0, half:N] = far[half:N]
    ring_send(1, 0, left)
    for s in (1, 2, 3):
        mine_r = part(hop(z, 4 - s, ZN))
        mine_l = part(hop(z, s - 4, ZN))
        for way, mine, dev in ((0, mine_r, right), (1, mine_l, left)):
            sbuf, rbuf = (zs_r, zr_r) if way == 0 else (zs_l, zr_l)
            ring(way, s - 1, dev).wait_recv()
            if s == 1:
                zs = slice(half * way, half * (way + 1))
                other = slice(half * (1 - way), half * (2 - way))
                sbuf[s, zs] = (mine[zs] + rbuf[0, zs].astype(F32)).astype(BF)
                sbuf[s, other] = mine[other].astype(BF)
            else:
                sbuf[s] = (mine + rbuf[s - 1].astype(F32)).astype(BF)
            ring_send(way, s, dev)
    own = part(z)
    ring(0, 3, right).wait_recv()
    ring(1, 3, left).wait_recv()
    out_ref[...] = (own + zr_r[3].astype(F32) + zr_l[3].astype(F32)).astype(BF)
    for c in sent:
        c.wait_send()


def on_device(node_feats, rel_weight, att_src, att_dst, src_row, dst_row):
    src = src_row.reshape(ZN, G, 16).transpose(1, 0, 2).reshape(G, 128)
    dst = dst_row.reshape(ZN, 128)
    vmem = pl.BlockSpec(memory_space=pltpu.VMEM)
    hbm = pl.BlockSpec(memory_space=pl.ANY)
    tile8 = pltpu.VMEM((8, 8, 128), F32)
    dma = pltpu.SemaphoreType.DMA
    return pl.pallas_call(
        kernel,
        out_shape=jax.ShapeDtypeStruct((N, CB), BF),
        in_specs=[hbm, hbm, vmem, vmem, vmem, vmem],
        out_specs=vmem,
        scratch_shapes=[
            pltpu.VMEM((N, D), BF),
            pltpu.VMEM((D, D), BF),
            pltpu.VMEM((RN, N, CB), BF),
            pltpu.VMEM((G, RN, N, CB), BF),
            pltpu.VMEM((RN, G, 128, N), BF),
            pltpu.VMEM((ZN, D, CB), BF),
            tile8, tile8,
            pltpu.VMEM((8, 128), F32),
            tile8,
            tile8, tile8, tile8, tile8, tile8, tile8,
            pltpu.VMEM((HEADS, 16, 128), F32),
            pltpu.VMEM((RN, 16, 128), F32),
            pltpu.VMEM((N, 128), F32),
            pltpu.VMEM((ZN, N, 128), BF),
            tile8,
            pltpu.VMEM((4, N, CB), BF),
            pltpu.VMEM((4, N, CB), BF),
            pltpu.VMEM((4, N, CB), BF),
            pltpu.VMEM((4, N, CB), BF),
            dma((2,)),
            dma((8,)), dma((8,)),
            dma((7, 8)), dma((7, 8)),
            dma((8,)), dma((8,)),
            dma((8,)), dma((8,)),
            dma((8,)), dma((8,)),
            dma((8,)), dma((8,)),
            dma((8,)), dma((8,)),
            dma((8,)), dma((8,)),
            dma((2, 4)), dma((2, 4)),
        ],
        compiler_params=pltpu.CompilerParams(
            collective_id=0, has_side_effects=True, vmem_limit_bytes=48 * 1024 * 1024
        ),
    )(node_feats, rel_weight[0], att_src, att_dst, src, dst)


def solution(mesh):
    placed = (
        P("dom", None),
        P("rel", None, None),
        P("rel", None),
        P("rel", None),
        P("rel", "dom", None, None),
        P("rel", "dom", None, None),
    )
    return jax.shard_map(
        on_device, mesh=mesh, in_specs=placed, out_specs=P("dom", "rel"), check_vma=False
    )
```

time: 153 us -> 72.2 us (0.47)
  waiting for transfers between devices: 83.2 us -> 0 us
  Pallas kernels: 0 us -> 65.4 us
  local copies, waits for them, and re-layouts: 21.7 us -> 6.36 us
  starting transfers between devices: 14.2 us -> 0 us
  between operations: 13.6 us -> 0.02 us
  other arithmetic: 12.3 us -> 0 us
  matrix products: 8 us -> 0 us
    pallas_call x0 -> x1, Pallas kernels: none -> 65.4 us  [on_device(): pl.pallas_call(kernel, out_shape=jax.ShapeDtypeStruct((N, CB), BF), in_sp...]
    all_to_all x1 -> x0, waiting for transfers between devices: 47.2 us -> none  [on_device(): lax.all_to_all(outgoing, 'dom', split_axis=0, concat_axis=0, tiled=True)]
    unnamed x2 -> x0, waiting for transfers between devices: 35.9 us -> none
    gather x7 -> x0, local copies, waits for them, and re-layouts: 14.4 us -> none  [the longest x1 5.39 us: on_device(): outgoing = own_proj[src_pick].reshape(peer_count, slot_cap, feat_width)]
    all_to_all x1 -> x0, starting transfers between devices: 14.1 us -> none  [on_device(): lax.all_to_all(outgoing, 'dom', split_axis=0, concat_axis=0, tiled=True)]
    dot_general x4 -> x0, matrix products: 8 us -> none  [the longest x1 3.31 us: on_device(): jnp.dot(edge_proj.astype(jnp.float32), head_matrix(att_src[0]), precision...]
    another operation x1 -> x0, other arithmetic: 6.08 us -> none  [on_device(): peak_score = jax.ops.segment_max(score, segment, node_rows + 1)]
    scatter-add x1 -> x0, other arithmetic: 6.08 us -> none  [on_device(): seg_total = jax.ops.segment_sum(expo, segment, node_rows + 1)]
  transfers between devices with their start and end apart: 2 -> 0, of which waited for: 2 -> 0; matrix products, arithmetic and copies ran while one was open for 3% -> 0% of each run, Pallas kernels for 0% -> 0%
where the time goes in v1:
time: 72.2 us; the launch traced here: 71.8 us
  Pallas kernels  65.4 us (91%)
  local copies, waits for them, and re-layouts  6.36 us (9%)
    pallas_call x1, Pallas kernels, on_device(): pl.pallas_call(kernel, out_shape=jax.ShapeDtypeStruct((N, CB), BF), in_sp...  65.4 us
    unnamed x11, local copies, waits for them, and re-layouts  6.2 us

profile of v1, /device:TPU:6, one launch (start us, length us, event | category | flops | bytes accessed | tf_op | source)
XLA Modules:
  0.0 71.8 jit_solution(6963637019722889704)
XLA Ops:
  0.0 0.8 %copy.9 = s32[1,1,64,16]{3,2,1,0:T(8,128)S(1)} copy(s32[1,1,64,16]{2,3,1,0:T(8,128)} %param.10) | data formatting | bytes 8192 | tf_op args[4]
  0.8 0.1 reshape.10.src_ref
  0.9 0.8 %copy.11 = s32[1,1,64,16]{3,2,1,0:T(8,128)S(1)} copy(s32[1,1,64,16]{2,3,1,0:T(8,128)} %param.11) | data formatting | bytes 8192 | tf_op args[5]
  1.6 0.1 reshape.11.dst_ref
  1.7 0.0 copy-start
  1.7 1.6 %copy-done = bf16[1,1024,1024]{2,1,0:T(8,128)(2,1)S(1)} copy-done((bf16[1,1024,1024]{2,1,0:T(8,128)(2,1)S(1)}, bf16[1,1024,1024]{2,1,0:T(8,128)(2,1)}, u32[]{:S(2)}) %copy-start) | copy-done | bytes 2097176
  3.3 0.0 copy-start.1
  3.3 1.0 %copy-done.1 = bf16[256,1024]{1,0:T(8,128)(2,1)S(1)} copy-done((bf16[256,1024]{1,0:T(8,128)(2,1)S(1)}, bf16[256,1024]{1,0:T(8,128)(2,1)}, u32[]{:S(2)}) %copy-start.1) | copy-done | bytes 524312
  4.4 0.0 copy-start.2
  4.4 0.7 copy-done.2
  5.1 0.0 copy-start.3
  5.1 0.7 copy-done.3
  5.7 65.4 %shard_map.64 = bf16[256,128]{1,0:T(8,128)(2,1)S(1)} custom-call(bf16[256,1024]{1,0:T(8,128)(2,1)S(1)} %copy-done.1, bf16[1024,1024]{1,0:T(8,128)(2,1)S(1)} %bitcast.6, f32[1,1024]{1,0:T(1,128)S(1)} %copy-done.2, f32[1,1024]{1,0:T(1,128)S(1)} %copy-done.3, s32[8,128]{1,0:T(8,128)S(1)} %reshape.10.src_ref, s32[8,128]{1,0:T(8,128)S(1)} %reshape.11.dst_ref), custom_call_target="tpu_custom_call" | custom-call | tf_op jit(solution)/shard_map/pallas_call | solution.py:372
  71.2 0.6 copy.13
  (1 shorter events, 0.0 us)
Async XLA Ops:
  1.7 1.6 %copy-start = (bf16[1,1024,1024]{2,1,0:T(8,128)(2,1)S(1)}, bf16[1,1024,1024]{2,1,0:T(8,128)(2,1)}, u32[]{:S(2)}) copy-start(bf16[1,1024,1024]{2,1,0:T(8,128)(2,1)} %param.7) | copy-start | bytes 6291460
  3.3 1.0 %copy-start.1 = (bf16[256,1024]{1,0:T(8,128)(2,1)S(1)}, bf16[256,1024]{1,0:T(8,128)(2,1)}, u32[]{:S(2)}) copy-start(bf16[256,1024]{1,0:T(8,128)(2,1)} %feat_ref.1) | copy-start | bytes 1572868
  4.4 0.7 copy-start.2
  5.1 0.7 copy-start.3

commit v2 on v1

--- a/solution.py
+++ b/solution.py
@@ -59,12 +59,12 @@
 
 
 def kernel(
-    feat_ref, w_ref, asrc_ref, adst_ref, src_ref, dst_ref, out_ref,
-    x_buf, w_buf, proj, pall, onehot, picked,
+    feat_ref, w_ref, asrc_hbm, adst_hbm, src_hbm, dst_hbm, out_ref,
+    x_buf, w_buf, asrc_ref, adst_ref, src_raw, dst_raw, src_ref, dst_ref, spread, proj, pall, onehot, picked,
     idx_send, idx_recv, idx_rows, idx_all,
     s1, r1, s2, r2, s3, r3, al_send, al_all,
     max_cols, dst_hot, expo,
-    zs_r, zs_l, zr_r, zr_l,
+    zs, zr,
     in_sem, y_ss, y_rs, x_ss, x_rs, g_ss, g_rs, h_ss, h_rs, k_ss, k_rs, m_ss, m_rs, n_ss, n_rs, o_ss, o_rs, z_ss, z_rs,
 ):
     r = lax.axis_index("rel")
@@ -73,8 +73,12 @@
     x, a = g // 2, g % 2
     load_x = pltpu.make_async_copy(feat_ref, x_buf, in_sem.at[0])
     load_w = pltpu.make_async_copy(w_ref, w_buf, in_sem.at[1])
-    load_x.start()
-    load_w.start()
+    load_src = pltpu.make_async_copy(src_hbm, src_raw, in_sem.at[2])
+    load_dst = pltpu.make_async_copy(dst_hbm, dst_raw, in_sem.at[3])
+    load_as = pltpu.make_async_copy(asrc_hbm, asrc_ref, in_sem.at[4])
+    load_ad = pltpu.make_async_copy(adst_hbm, adst_ref, in_sem.at[5])
+    for load in (load_src, load_dst, load_x, load_w, load_as, load_ad):
+        load.start()
 
     def in_group(i):
         return (r, z * G + i)
@@ -92,6 +96,23 @@
     for d in range(1, 8):
         for dev in (in_group(hop(g, d, G)), in_z(hop(z, d, ZN)), in_rel(hop(r, d, RN))):
             pl.semaphore_signal(barrier, inc=1, device_id=dev, device_id_type=MESH)
+
+    lane_block = lax.broadcasted_iota(jnp.int32, (8, 128), 1) // 16
+    load_src.wait()
+    spread[...] = jnp.concatenate([src_raw[...].astype(F32)] * 8, axis=0).T
+    src_f = jnp.zeros((8, 128), F32)
+    for i in range(ZN):
+        src_f = jnp.where(lane_block == i, spread[8 * i : 8 * i + 8, :], src_f)
+    src_ref[...] = src_f.astype(jnp.int32)
+    load_dst.wait()
+    spread[...] = jnp.concatenate([dst_raw[...].astype(F32)] * 8, axis=0).T
+    dst_f = jnp.zeros((8, 128), F32)
+    for i in range(G):
+        dst_f = jnp.where(lane_block == i, spread[pl.ds(i, 8, stride=8), :], dst_f)
+    dst_ref[...] = dst_f.astype(jnp.int32)
+    idx_rows[...] = src_f
+    idx_all[0] = src_f
+
     pl.semaphore_wait(barrier, 21)
 
     sent = []
@@ -108,7 +129,7 @@
 
     def exchange(sbuf, rbuf, ss, rs, me, member):
         rbuf[me] = sbuf[me]
-        for d in range(1, 8):
+        for d in ORDER[:0:-1]:
             to = hop(me, d, 8)
             send(sbuf.at[to], rbuf.at[me], ss.at[d], rs.at[8 - d], member(to))
 
@@ -117,10 +138,8 @@
             frm = hop(me, d, 8)
             copy(sbuf.at[frm], rbuf.at[frm], ss.at[d], rs.at[d], member(frm)).wait_recv()
 
-    src_f = src_ref[...].astype(F32)
-    for i in range(G):
-        idx_send[i] = jnp.broadcast_to(src_f[i : i + 1], (8, 128))
-    exchange(idx_send, idx_recv, g_ss, g_rs, g, in_group)
+    for d in ORDER[:0:-1]:
+        send(idx_rows, idx_all.at[8 - d], h_ss.at[d], h_rs.at[8 - d], in_rel(hop(r, d, RN)))
 
     load_x.wait()
     load_w.wait()
@@ -129,13 +148,6 @@
         part = dot(feats, w_buf[:, 256 * i : 256 * (i + 1)]).astype(BF)
         proj[2 * i] = part[:, :CB]
         proj[2 * i + 1] = part[:, CB:]
-
-    arrived(idx_send, idx_recv, g_ss, g_rs, g, in_group)
-    for i in range(G):
-        idx_rows[i : i + 1, :] = idx_recv[i, 0:1, :]
-    idx_all[0] = idx_rows[...]
-    for d in range(1, 8):
-        send(idx_rows, idx_all.at[8 - d], h_ss.at[d], h_rs.at[8 - d], in_rel(hop(r, d, RN)))
 
     pall[g, 0] = proj[r]
     for d in ORDER[1:]:
@@ -179,15 +191,15 @@
         got(5, j, 2 * x_r + 1 - a)
         got(6, j, 2 * x_2 + 1 - a)
 
-        def body(i, carry):
+        for i in range(G):
             rows = dot(onehot[j, i], pall[i, j]).astype(BF)
-            picked[:, pl.ds(pl.multiple_of(j * 128 + i * 16, 16), 16), :] = rows.reshape(ZN, 16, CB)
-            return carry
-
-        lax.fori_loop(0, G, body, 0)
+            k = j * 128 + i * 16
+            picked[:, k : k + 16, :] = rows.reshape(ZN, 16, CB)
 
     stage_own(0)
 
+    load_as.wait()
+    load_ad.wait()
     row8 = lax.broadcasted_iota(jnp.int32, (8, D), 0)
     lane8 = lax.broadcasted_iota(jnp.int32, (8, D), 1)
     att = jnp.where(row8 < HEADS, asrc_ref[...], adst_ref[...])
@@ -205,27 +217,36 @@
         s1[i] = join3(dot(score3, hot))
     exchange(s1, r1, k_ss, k_rs, g, in_group)
 
+    for d in range(1, 8):
+        copy(idx_rows, idx_all.at[d], h_ss.at[d], h_rs.at[d], in_rel(hop(r, d, RN))).wait_recv()
+    for i in range(G):
+        idx_send[i] = idx_all[:, i, :]
+    exchange(idx_send, idx_recv, g_ss, g_rs, g, in_group)
+
     stage_own(1)
+    stage_own(7)
 
     arrived(s1, r1, k_ss, k_rs, g, in_group)
     for i, tile in enumerate(block_transpose([r1[i] for i in range(G)])):
         s2[i] = tile
     exchange(s2, r2, m_ss, m_rs, z, in_z)
 
-    stage_own(7)
     stage_near(0)
-
-    for d in range(1, 8):
-        copy(idx_rows, idx_all.at[d], h_ss.at[d], h_rs.at[d], in_rel(hop(r, d, RN))).wait_recv()
+    stage_own(2)
+    stage_own(6)
+    stage_near(1)
+    stage_near(7)
+
+    arrived(idx_send, idx_recv, g_ss, g_rs, g, in_group)
     iota_l = lax.broadcasted_iota(jnp.int32, (128, N), 1).astype(F32)
 
-    def hot_body(j, carry):
-        cols = idx_all[j].T
-        for i in range(G):
-            onehot[j, i] = jnp.where(cols[:, i : i + 1] == iota_l, 1.0, 0.0).astype(BF)
+    def hot_body(i, carry):
+        cols = idx_recv[i].T
+        for j in range(RN):
+            onehot[j, i] = jnp.where(cols[:, j : j + 1] == iota_l, 1.0, 0.0).astype(BF)
         return carry
 
-    lax.fori_loop(0, RN, hot_body, 0)
+    lax.fori_loop(0, G, hot_body, 0)
 
     arrived(s2, r2, m_ss, m_rs, z, in_z)
     row = lax.broadcasted_iota(jnp.int32, (8, 128), 0)
@@ -269,37 +290,33 @@
         s3[i] = jnp.where(row == HEADS, dst_ref[i : i + 1, :].astype(F32), alpha)
     exchange(s3, r3, n_ss, n_rs, z, in_z)
 
-    stage_own(2)
-    stage_near(1)
-    stage_own(6)
+    stage_own(3)
+    stage_own(5)
+    stage_near(2)
+    stage_own(4)
+    stage_near(6)
+    stage_far(0)
+    stage_far(1)
+    stage_far(7)
+    stage_near(3)
+    stage_pick(0)
+    stage_near(5)
+    stage_far(2)
+    stage_pick(1)
+    stage_pick(7)
 
     arrived(s3, r3, n_ss, n_rs, z, in_z)
     for h in range(HEADS):
         al_send[h, 0:8] = r3[:, h, :]
         al_send[h, 8:16] = r3[:, HEADS, :]
     al_all[0] = al_send[r // 2]
-    for d in range(1, 8):
+    for d in ORDER[:0:-1]:
         to = hop(r, d, RN)
         send(al_send.at[to // 2], al_all.at[8 - d], o_ss.at[d], o_rs.at[8 - d], in_rel(to))
 
-    stage_near(7)
-    stage_far(0)
-    stage_own(3)
-    stage_near(2)
-    stage_far(1)
-    stage_own(5)
-    stage_pick(0)
-    stage_near(6)
-    stage_far(7)
-    stage_own(4)
-    stage_pick(1)
-    stage_near(3)
-    stage_far(2)
-    stage_pick(7)
-    stage_near(5)
+    stage_near(4)
     stage_far(6)
     stage_pick(2)
-    stage_near(4)
     stage_far(3)
     stage_pick(6)
     stage_far(5)
@@ -322,61 +339,71 @@
             acc = acc + dot(jnp.concatenate(both, axis=1), picked[zt, j * 128 : j * 128 + 256, :])
         return acc
 
-    right, left = in_z(hop(z, 1, ZN)), in_z(hop(z, -1, ZN))
     half = N // 2
 
-    def ring(way, s, dev):
-        sbuf, rbuf = (zs_r, zr_r) if way == 0 else (zs_l, zr_l)
-        rows = pl.ds(half * way, half) if s == 0 else pl.ds(0, N)
-        return copy(sbuf.at[s, rows], rbuf.at[s, rows], z_ss.at[way, s], z_rs.at[way, s], dev)
-
-    def ring_send(way, s, dev):
-        c = ring(way, s, dev)
+    def ring(way, kind):
+        to = hop(z, (1 if way == 0 else -1) * (1, 2, 1, 2)[kind], ZN)
+        rows = pl.ds(half * way, half) if kind == 1 else pl.ds(0, N)
+        return copy(
+            zs.at[way, kind, rows], zr.at[way, kind, rows], z_ss.at[way, kind], z_rs.at[way, kind], in_z(to)
+        )
+
+    def ring_send(way, kind):
+        c = ring(way, kind)
         c.start()
         sent.append(c)
 
+    for way, sign in ((0, 1), (1, -1)):
+        zs[way, 0] = part(hop(z, 3 * sign, ZN)).astype(BF)
+        ring_send(way, 0)
     far = part(hop(z, 4, ZN)).astype(BF)
-    zs_r[0, 0:half] = far[0:half]
-    ring_send(0, 0, right)
-    zs_l[0, half:N] = far[half:N]
-    ring_send(1, 0, left)
-    for s in (1, 2, 3):
-        mine_r = part(hop(z, 4 - s, ZN))
-        mine_l = part(hop(z, s - 4, ZN))
-        for way, mine, dev in ((0, mine_r, right), (1, mine_l, left)):
-            sbuf, rbuf = (zs_r, zr_r) if way == 0 else (zs_l, zr_l)
-            ring(way, s - 1, dev).wait_recv()
-            if s == 1:
-                zs = slice(half * way, half * (way + 1))
-                other = slice(half * (1 - way), half * (2 - way))
-                sbuf[s, zs] = (mine[zs] + rbuf[0, zs].astype(F32)).astype(BF)
-                sbuf[s, other] = mine[other].astype(BF)
-            else:
-                sbuf[s] = (mine + rbuf[s - 1].astype(F32)).astype(BF)
-            ring_send(way, s, dev)
+    for way in (0, 1):
+        rows = slice(half * way, half * (way + 1))
+        zs[way, 1, rows] = far[rows]
+        ring_send(way, 1)
+    for way, sign in ((0, 1), (1, -1)):
+        zs[way, 2] = part(hop(z, sign, ZN)).astype(BF)
+        ring_send(way, 2)
+    mine = [part(hop(z, 2 * sign, ZN)) for sign in (1, -1)]
     own = part(z)
-    ring(0, 3, right).wait_recv()
-    ring(1, 3, left).wait_recv()
-    out_ref[...] = (own + zr_r[3].astype(F32) + zr_l[3].astype(F32)).astype(BF)
+    for way in (0, 1):
+        ring(way, 0).wait_recv()
+        ring(way, 1).wait_recv()
+        rows = slice(half * way, half * (way + 1))
+        other = slice(half * (1 - way), half * (2 - way))
+        zs[way, 3, rows] = (mine[way][rows] + zr[way, 0, rows].astype(F32) + zr[way, 1, rows].astype(F32)).astype(BF)
+        zs[way, 3, other] = (mine[way][other] + zr[way, 0, other].astype(F32)).astype(BF)
+        ring_send(way, 3)
+    for way in (0, 1):
+        ring(way, 2).wait_recv()
+        own = own + zr[way, 2].astype(F32)
+    for way in (0, 1):
+        ring(way, 3).wait_recv()
+        own = own + zr[way, 3].astype(F32)
+    out_ref[...] = own.astype(BF)
     for c in sent:
         c.wait_send()
 
 
 def on_device(node_feats, rel_weight, att_src, att_dst, src_row, dst_row):
-    src = src_row.reshape(ZN, G, 16).transpose(1, 0, 2).reshape(G, 128)
-    dst = dst_row.reshape(ZN, 128)
+    src = src_row.reshape(64, 16).T
+    dst = dst_row.reshape(64, 16).T
     vmem = pl.BlockSpec(memory_space=pltpu.VMEM)
-    hbm = pl.BlockSpec(memory_space=pl.ANY)
+    hbm = pl.BlockSpec(memory_space=pltpu.HBM)
     tile8 = pltpu.VMEM((8, 8, 128), F32)
     dma = pltpu.SemaphoreType.DMA
     return pl.pallas_call(
         kernel,
         out_shape=jax.ShapeDtypeStruct((N, CB), BF),
-        in_specs=[hbm, hbm, vmem, vmem, vmem, vmem],
+        in_specs=[hbm] * 6,
         out_specs=vmem,
         scratch_shapes=[
             pltpu.VMEM((N, D), BF),
             pltpu.VMEM((D, D), BF),
+            pltpu.VMEM((1, D), F32), pltpu.VMEM((1, D), F32),
+            pltpu.VMEM((16, 64), jnp.int32), pltpu.VMEM((16, 64), jnp.int32),
+            pltpu.VMEM((8, 128), jnp.int32), pltpu.VMEM((8, 128), jnp.int32),
+            pltpu.VMEM((64, 128), F32),
             pltpu.VMEM((RN, N, CB), BF),
             pltpu.VMEM((G, RN, N, CB), BF),
             pltpu.VMEM((RN, G, 128, N), BF),
@@ -390,11 +417,9 @@
             pltpu.VMEM((N, 128), F32),
             pltpu.VMEM((ZN, N, 128), BF),
             tile8,
-            pltpu.VMEM((4, N, CB), BF),
-            pltpu.VMEM((4, N, CB), BF),
-            pltpu.VMEM((4, N, CB), BF),
-            pltpu.VMEM((4, N, CB), BF),
-            dma((2,)),
+            pltpu.VMEM((2, 4, N, CB), BF),
+            pltpu.VMEM((2, 4, N, CB), BF),
+            dma((6,)),
             dma((8,)), dma((8,)),
             dma((7, 8)), dma((7, 8)),
             dma((8,)), dma((8,)),
@@ -406,7 +431,7 @@
             dma((2, 4)), dma((2, 4)),
         ],
         compiler_params=pltpu.CompilerParams(
-            collective_id=0, has_side_effects=True, vmem_limit_bytes=48 * 1024 * 1024
+            collective_id=0, has_side_effects=True, vmem_limit_bytes=62 * 1024 * 1024
         ),
     )(node_feats, rel_weight[0], att_src, att_dst, src, dst)
 

time: 72.2 us -> 56.3 us (0.78)
  Pallas kernels: 65.4 us -> 53.8 us
  local copies, waits for them, and re-layouts: 6.36 us -> 1.47 us
    pallas_call x1, Pallas kernels: 65.4 us -> 53.8 us  [on_device(): pl.pallas_call(kernel, out_shape=jax.ShapeDtypeStruct((N, CB), BF), in_sp...]
    unnamed x11 -> x1, local copies, waits for them, and re-layouts: 6.2 us -> 1.47 us
where the time goes in v2:
time: 56.3 us; the launch traced here: 55.3 us
  Pallas kernels  53.8 us (96%)
  local copies, waits for them, and re-layouts  1.47 us (3%)
    pallas_call x1, Pallas kernels, on_device(): pl.pallas_call(kernel, out_shape=jax.ShapeDtypeStruct((N, CB), BF), in_sp...  53.8 us
    unnamed x1, local copies, waits for them, and re-layouts  1.47 us

profile of v2, /device:TPU:6, one launch (start us, length us, event | category | flops | bytes accessed | tf_op | source)
XLA Modules:
  0.0 55.3 jit_solution(10848954989656813086)
XLA Ops:
  0.0 53.8 %shard_map.64 = bf16[256,128]{1,0:T(8,128)(2,1)} custom-call(bf16[256,1024]{1,0:T(8,128)(2,1)} %feat_ref.1, bf16[1024,1024]{1,0:T(8,128)(2,1)} %bitcast.7, f32[1,1024]{1,0:T(1,128)} %asrc_hbm.1, f32[1,1024]{1,0:T(1,128)} %adst_hbm.1, s32[16,64]{1,0:T(8,128)} %bitcast.8, s32[16,64]{1,0:T(8,128)} %bitcast.9), custom_call_target="tpu_custom_call" | custom-call | tf_op jit(solution)/shard_map/pallas_call | solution.py:395
  53.8 1.5 %copy.8 = bf16[256,128]{1,0:T(8,128)(2,1)} copy(bf16[256,128]{1,0:T(8,128)(2,1)} %shard_map.64) | data formatting | bytes 131072

commit v3 on v2

--- a/solution.py
+++ b/solution.py
@@ -65,19 +65,22 @@
     s1, r1, s2, r2, s3, r3, al_send, al_all,
     max_cols, dst_hot, expo,
     zs, zr,
-    in_sem, y_ss, y_rs, x_ss, x_rs, g_ss, g_rs, h_ss, h_rs, k_ss, k_rs, m_ss, m_rs, n_ss, n_rs, o_ss, o_rs, z_ss, z_rs,
+    in_sem, w_sem, y_ss, y_rs, x_ss, x_rs, g_ss, g_rs, h_ss, h_rs, k_ss, k_rs, m_ss, m_rs, n_ss, n_rs, o_ss, o_rs, z_ss, z_rs,
 ):
     r = lax.axis_index("rel")
     p = lax.axis_index("dom")
     z, g = p // G, p % G
     x, a = g // 2, g % 2
     load_x = pltpu.make_async_copy(feat_ref, x_buf, in_sem.at[0])
-    load_w = pltpu.make_async_copy(w_ref, w_buf, in_sem.at[1])
+    load_w = [
+        pltpu.make_async_copy(w_ref.at[:, 256 * i : 256 * (i + 1)], w_buf.at[:, 256 * i : 256 * (i + 1)], w_sem.at[i])
+        for i in range(4)
+    ]
     load_src = pltpu.make_async_copy(src_hbm, src_raw, in_sem.at[2])
     load_dst = pltpu.make_async_copy(dst_hbm, dst_raw, in_sem.at[3])
     load_as = pltpu.make_async_copy(asrc_hbm, asrc_ref, in_sem.at[4])
     load_ad = pltpu.make_async_copy(adst_hbm, adst_ref, in_sem.at[5])
-    for load in (load_src, load_dst, load_x, load_w, load_as, load_ad):
+    for load in (load_x, *load_w, load_src, load_dst, load_as, load_ad):
         load.start()
 
     def in_group(i):
@@ -113,8 +116,6 @@
     idx_rows[...] = src_f
     idx_all[0] = src_f
 
-    pl.semaphore_wait(barrier, 21)
-
     sent = []
 
     def copy(src, dst, ss, rs, dev):
@@ -138,21 +139,25 @@
             frm = hop(me, d, 8)
             copy(sbuf.at[frm], rbuf.at[frm], ss.at[d], rs.at[d], member(frm)).wait_recv()
 
-    for d in ORDER[:0:-1]:
-        send(idx_rows, idx_all.at[8 - d], h_ss.at[d], h_rs.at[8 - d], in_rel(hop(r, d, RN)))
-
     load_x.wait()
-    load_w.wait()
     feats = x_buf[...]
     for i in range(4):
+        load_w[i].wait()
         part = dot(feats, w_buf[:, 256 * i : 256 * (i + 1)]).astype(BF)
         proj[2 * i] = part[:, :CB]
         proj[2 * i + 1] = part[:, CB:]
 
+    pl.semaphore_wait(barrier, 21)
+
+    for d in ORDER[:0:-1]:
+        send(idx_rows, idx_all.at[8 - d], h_ss.at[d], h_rs.at[8 - d], in_rel(hop(r, d, RN)))
     pall[g, 0] = proj[r]
-    for d in ORDER[1:]:
-        to = hop(r, d, RN)
-        send(proj.at[to], pall.at[g, 8 - d], y_ss.at[d], y_rs.at[8 - d], in_rel(to))
+    def y_send(*ds):
+        for d in ds:
+            to = hop(r, d, RN)
+            send(proj.at[to], pall.at[g, 8 - d], y_ss.at[d], y_rs.at[8 - d], in_rel(to))
+
+    y_send(1, 7, 2, 6)
 
     x_r, x_l, x_2 = hop(x, 1, 4), hop(x, 3, 4), hop(x, 2, 4)
     g_r, g_l, g_2 = 2 * x_r + a, 2 * x_l + a, 2 * x_2 + a
@@ -196,100 +201,118 @@
             k = j * 128 + i * 16
             picked[:, k : k + 16, :] = rows.reshape(ZN, 16, CB)
 
+
+    def scores():
+        load_as.wait()
+        load_ad.wait()
+        row8 = lax.broadcasted_iota(jnp.int32, (8, D), 0)
+        lane8 = lax.broadcasted_iota(jnp.int32, (8, D), 1)
+        att = jnp.where(row8 < HEADS, asrc_ref[...], adst_ref[...])
+        att = split3(jnp.where(lane8 // (D // HEADS) == row8 % HEADS, att, 0.0))
+        total = jnp.zeros((32, N), F32)
+        for c in range(RN):
+            total = total + dot_nt(att[:, CB * c : CB * (c + 1)], proj[c])
+        score = join3(total)
+        score3 = split3(score)
+
+        iota_n = lax.broadcasted_iota(jnp.int32, (N, 128), 0)
+        src_i = src_ref[...]
+        for i in range(G):
+            hot = jnp.where(src_i[i : i + 1] == iota_n, 1.0, 0.0).astype(BF)
+            s1[i] = join3(dot(score3, hot))
+
+        exchange(s1, r1, k_ss, k_rs, g, in_group)
+        return score, iota_n
+
+    def rows_to_group():
+        for d in range(1, 8):
+            copy(idx_rows, idx_all.at[d], h_ss.at[d], h_rs.at[d], in_rel(hop(r, d, RN))).wait_recv()
+        for i in range(G):
+            idx_send[i] = idx_all[:, i, :]
+        exchange(idx_send, idx_recv, g_ss, g_rs, g, in_group)
+
+    def scores_along_z():
+        arrived(s1, r1, k_ss, k_rs, g, in_group)
+        for i, tile in enumerate(block_transpose([r1[i] for i in range(G)])):
+            s2[i] = tile
+        exchange(s2, r2, m_ss, m_rs, z, in_z)
+
+    def hot_wait():
+        arrived(idx_send, idx_recv, g_ss, g_rs, g, in_group)
+
+    def hot(i):
+        iota_l = lax.broadcasted_iota(jnp.int32, (128, N), 1).astype(F32)
+        cols = idx_recv[i].T
+        for j in range(RN):
+            onehot[j, i] = jnp.where(cols[:, j : j + 1] == iota_l, 1.0, 0.0).astype(BF)
+
+    def softmax():
+        arrived(s2, r2, m_ss, m_rs, z, in_z)
+        row = lax.broadcasted_iota(jnp.int32, (8, 128), 0)
+        lane = lax.broadcasted_iota(jnp.int32, (64, 128), 1)
+        neg = -jnp.inf
+
+        def max_body(t, carry):
+            base = pl.multiple_of(t * 64, 64)
+            iota_t = lax.broadcasted_iota(jnp.int32, (64, 128), 0) + base
+            best = [jnp.full((64, 128), neg, F32) for _ in range(HEADS)]
+            for i in range(ZN):
+                mask = dst_ref[i : i + 1, :] == iota_t
+                dst_hot[i, pl.ds(base, 64), :] = jnp.where(mask, 1.0, 0.0).astype(BF)
+                for h in range(HEADS):
+                    best[h] = jnp.maximum(best[h], jnp.where(mask, r2[i, h : h + 1, :], neg))
+            cols = jnp.zeros((64, 128), F32)
+            for h in range(HEADS):
+                cols = jnp.where(lane == h, jnp.max(best[h], axis=1, keepdims=True), cols)
+            max_cols[pl.ds(base, 64), :] = cols
+            return carry
+
+        lax.fori_loop(0, 4, max_body, 0)
+        peak_src = max_cols[...].T[0:8]
+        row_n = lax.broadcasted_iota(jnp.int32, (8, N), 0)
+        dst_up = pltpu.roll(score, 4, 0)
+        peak = jnp.where(peak_src == neg, 0.0, leaky(peak_src + dst_up))
+        table = split3(jnp.where(row_n < HEADS, peak, score))
+        seg = jnp.zeros((32, N), F32)
+        for i in range(ZN):
+            near = join3(dot(table, dst_hot[i]))
+            edge = leaky(r2[i] + pltpu.roll(near, 4, 0))
+            live = (row < HEADS) & (dst_ref[i : i + 1, :] >= 0)
+            e = jnp.where(live, jnp.exp(jnp.where(live, edge - near, 0.0)), 0.0)
+            expo[i] = e
+            seg = seg + dot_nt(split3(e), dst_hot[i])
+        seg3 = split3(join3(seg))
+        for i in range(ZN):
+            live = (row < HEADS) & (dst_ref[i : i + 1, :] >= 0)
+            under = jnp.where(live, join3(dot(seg3, dst_hot[i])), 1.0)
+            alpha = jnp.where(live, expo[i] / under, 0.0)
+            s3[i] = jnp.where(row == HEADS, dst_ref[i : i + 1, :].astype(F32), alpha)
+        exchange(s3, r3, n_ss, n_rs, z, in_z)
+
+    def coefficients():
+        arrived(s3, r3, n_ss, n_rs, z, in_z)
+        for h in range(HEADS):
+            al_send[h, 0:8] = r3[:, h, :]
+            al_send[h, 8:16] = r3[:, HEADS, :]
+        al_all[0] = al_send[r // 2]
+        for d in ORDER[:0:-1]:
+            to = hop(r, d, RN)
+            send(al_send.at[to // 2], al_all.at[8 - d], o_ss.at[d], o_rs.at[8 - d], in_rel(to))
+
     stage_own(0)
-
-    load_as.wait()
-    load_ad.wait()
-    row8 = lax.broadcasted_iota(jnp.int32, (8, D), 0)
-    lane8 = lax.broadcasted_iota(jnp.int32, (8, D), 1)
-    att = jnp.where(row8 < HEADS, asrc_ref[...], adst_ref[...])
-    att = split3(jnp.where(lane8 // (D // HEADS) == row8 % HEADS, att, 0.0))
-    total = jnp.zeros((32, N), F32)
-    for c in range(RN):
-        total = total + dot_nt(att[:, CB * c : CB * (c + 1)], proj[c])
-    score = join3(total)
-    score3 = split3(score)
-
-    iota_n = lax.broadcasted_iota(jnp.int32, (N, 128), 0)
-    src_i = src_ref[...]
-    for i in range(G):
-        hot = jnp.where(src_i[i : i + 1] == iota_n, 1.0, 0.0).astype(BF)
-        s1[i] = join3(dot(score3, hot))
-    exchange(s1, r1, k_ss, k_rs, g, in_group)
-
-    for d in range(1, 8):
-        copy(idx_rows, idx_all.at[d], h_ss.at[d], h_rs.at[d], in_rel(hop(r, d, RN))).wait_recv()
-    for i in range(G):
-        idx_send[i] = idx_all[:, i, :]
-    exchange(idx_send, idx_recv, g_ss, g_rs, g, in_group)
-
+    score, iota_n = scores()
+    rows_to_group()
     stage_own(1)
     stage_own(7)
-
-    arrived(s1, r1, k_ss, k_rs, g, in_group)
-    for i, tile in enumerate(block_transpose([r1[i] for i in range(G)])):
-        s2[i] = tile
-    exchange(s2, r2, m_ss, m_rs, z, in_z)
-
+    y_send(3,5)
+    scores_along_z()
     stage_near(0)
     stage_own(2)
     stage_own(6)
+    y_send(4)
     stage_near(1)
     stage_near(7)
-
-    arrived(idx_send, idx_recv, g_ss, g_rs, g, in_group)
-    iota_l = lax.broadcasted_iota(jnp.int32, (128, N), 1).astype(F32)
-
-    def hot_body(i, carry):
-        cols = idx_recv[i].T
-        for j in range(RN):
-            onehot[j, i] = jnp.where(cols[:, j : j + 1] == iota_l, 1.0, 0.0).astype(BF)
-        return carry
-
-    lax.fori_loop(0, G, hot_body, 0)
-
-    arrived(s2, r2, m_ss, m_rs, z, in_z)
-    row = lax.broadcasted_iota(jnp.int32, (8, 128), 0)
-    lane = lax.broadcasted_iota(jnp.int32, (64, 128), 1)
-    neg = -jnp.inf
-
-    def max_body(t, carry):
-        base = pl.multiple_of(t * 64, 64)
-        iota_t = lax.broadcasted_iota(jnp.int32, (64, 128), 0) + base
-        best = [jnp.full((64, 128), neg, F32) for _ in range(HEADS)]
-        for i in range(ZN):
-            mask = dst_ref[i : i + 1, :] == iota_t
-            dst_hot[i, pl.ds(base, 64), :] = jnp.where(mask, 1.0, 0.0).astype(BF)
-            for h in range(HEADS):
-                best[h] = jnp.maximum(best[h], jnp.where(mask, r2[i, h : h + 1, :], neg))
-        cols = jnp.zeros((64, 128), F32)
-        for h in range(HEADS):
-            cols = jnp.where(lane == h, jnp.max(best[h], axis=1, keepdims=True), cols)
-        max_cols[pl.ds(base, 64), :] = cols
-        return carry
-
-    lax.fori_loop(0, 4, max_body, 0)
-    peak_src = max_cols[...].T[0:8]
-    row_n = lax.broadcasted_iota(jnp.int32, (8, N), 0)
-    dst_up = pltpu.roll(score, 4, 0)
-    peak = jnp.where(peak_src == neg, 0.0, leaky(peak_src + dst_up))
-    table = split3(jnp.where(row_n < HEADS, peak, score))
-    seg = jnp.zeros((32, N), F32)
-    for i in range(ZN):
-        near = join3(dot(table, dst_hot[i]))
-        edge = leaky(r2[i] + pltpu.roll(near, 4, 0))
-        live = (row < HEADS) & (dst_ref[i : i + 1, :] >= 0)
-        e = jnp.where(live, jnp.exp(jnp.where(live, edge - near, 0.0)), 0.0)
-        expo[i] = e
-        seg = seg + dot_nt(split3(e), dst_hot[i])
-    seg3 = split3(join3(seg))
-    for i in range(ZN):
-        live = (row < HEADS) & (dst_ref[i : i + 1, :] >= 0)
-        under = jnp.where(live, join3(dot(seg3, dst_hot[i])), 1.0)
-        alpha = jnp.where(live, expo[i] / under, 0.0)
-        s3[i] = jnp.where(row == HEADS, dst_ref[i : i + 1, :].astype(F32), alpha)
-    exchange(s3, r3, n_ss, n_rs, z, in_z)
-
+    softmax()
     stage_own(3)
     stage_own(5)
     stage_near(2)
@@ -299,21 +322,15 @@
     stage_far(1)
     stage_far(7)
     stage_near(3)
+    hot_wait()
+    for i in range(G):
+        hot(i)
     stage_pick(0)
     stage_near(5)
     stage_far(2)
     stage_pick(1)
     stage_pick(7)
-
-    arrived(s3, r3, n_ss, n_rs, z, in_z)
-    for h in range(HEADS):
-        al_send[h, 0:8] = r3[:, h, :]
-        al_send[h, 8:16] = r3[:, HEADS, :]
-    al_all[0] = al_send[r // 2]
-    for d in ORDER[:0:-1]:
-        to = hop(r, d, RN)
-        send(al_send.at[to // 2], al_all.at[8 - d], o_ss.at[d], o_rs.at[8 - d], in_rel(to))
-
+    coefficients()
     stage_near(4)
     stage_far(6)
     stage_pick(2)
@@ -341,11 +358,15 @@
 
     half = N // 2
 
+    spans = ((0, half), (half, half))
+
     def ring(way, kind):
-        to = hop(z, (1 if way == 0 else -1) * (1, 2, 1, 2)[kind], ZN)
-        rows = pl.ds(half * way, half) if kind == 1 else pl.ds(0, N)
+        to = hop(z, (1 if way == 0 else -1) * (1, 1, 2, 1, 2, 2)[kind], ZN)
+        shared, alone = spans[way], spans[1 - way]
+        rows = pl.ds(*(alone, shared, shared, (0, N), alone, shared)[kind])
+        slot = (0, 0, 1, 2, 3, 3)[kind]
         return copy(
-            zs.at[way, kind, rows], zr.at[way, kind, rows], z_ss.at[way, kind], z_rs.at[way, kind], in_z(to)
+            zs.at[way, slot, rows], zr.at[way, slot, rows], z_ss.at[way, kind], z_rs.at[way, kind], in_z(to)
         )
 
     def ring_send(way, kind):
@@ -356,29 +377,35 @@
     for way, sign in ((0, 1), (1, -1)):
         zs[way, 0] = part(hop(z, 3 * sign, ZN)).astype(BF)
         ring_send(way, 0)
+        ring_send(way, 1)
     far = part(hop(z, 4, ZN)).astype(BF)
     for way in (0, 1):
         rows = slice(half * way, half * (way + 1))
         zs[way, 1, rows] = far[rows]
-        ring_send(way, 1)
+        ring_send(way, 2)
     for way, sign in ((0, 1), (1, -1)):
         zs[way, 2] = part(hop(z, sign, ZN)).astype(BF)
-        ring_send(way, 2)
+        ring_send(way, 3)
     mine = [part(hop(z, 2 * sign, ZN)) for sign in (1, -1)]
+    for way in (0, 1):
+        ring(way, 0).wait_recv()
+        rows = slice(half * (1 - way), half * (2 - way))
+        zs[way, 3, rows] = (mine[way][rows] + zr[way, 0, rows].astype(F32)).astype(BF)
+        ring_send(way, 4)
     own = part(z)
     for way in (0, 1):
-        ring(way, 0).wait_recv()
         ring(way, 1).wait_recv()
+        ring(way, 2).wait_recv()
         rows = slice(half * way, half * (way + 1))
-        other = slice(half * (1 - way), half * (2 - way))
         zs[way, 3, rows] = (mine[way][rows] + zr[way, 0, rows].astype(F32) + zr[way, 1, rows].astype(F32)).astype(BF)
-        zs[way, 3, other] = (mine[way][other] + zr[way, 0, other].astype(F32)).astype(BF)
-        ring_send(way, 3)
-    for way in (0, 1):
-        ring(way, 2).wait_recv()
+        ring_send(way, 5)
+    for way in (0, 1):
+        ring(way, 3).wait_recv()
         own = own + zr[way, 2].astype(F32)
     for way in (0, 1):
-        ring(way, 3).wait_recv()
+        ring(way, 4).wait_recv()
+    for way in (0, 1):
+        ring(way, 5).wait_recv()
         own = own + zr[way, 3].astype(F32)
     out_ref[...] = own.astype(BF)
     for c in sent:
@@ -394,7 +421,7 @@
     dma = pltpu.SemaphoreType.DMA
     return pl.pallas_call(
         kernel,
-        out_shape=jax.ShapeDtypeStruct((N, CB), BF),
+        out_shape=pltpu.VMEM((N, CB), BF),
         in_specs=[hbm] * 6,
         out_specs=vmem,
         scratch_shapes=[
@@ -419,7 +446,7 @@
             tile8,
             pltpu.VMEM((2, 4, N, CB), BF),
             pltpu.VMEM((2, 4, N, CB), BF),
-            dma((6,)),
+            dma((6,)), dma((4,)),
             dma((8,)), dma((8,)),
             dma((7, 8)), dma((7, 8)),
             dma((8,)), dma((8,)),
@@ -428,7 +455,7 @@
             dma((8,)), dma((8,)),
             dma((8,)), dma((8,)),
             dma((8,)), dma((8,)),
-            dma((2, 4)), dma((2, 4)),
+            dma((2, 6)), dma((2, 6)),
         ],
         compiler_params=pltpu.CompilerParams(
             collective_id=0, has_side_effects=True, vmem_limit_bytes=62 * 1024 * 1024

time: 56.3 us -> 52.8 us (0.938); the launches traced: 55.3 us -> 52.4 us
  Pallas kernels: 53.8 us -> 51.7 us
  local copies, waits for them, and re-layouts: 1.47 us -> 0.63 us
    pallas_call x1, Pallas kernels: 53.8 us -> 51.7 us  [on_device(): pl.pallas_call(kernel, out_shape=pltpu.VMEM((N, CB), BF), in_specs=[hbm]...]
    unnamed x1, local copies, waits for them, and re-layouts: 1.47 us -> 0.63 us
where the time goes in v3:
time: 52.8 us; the launch traced here: 52.4 us
  Pallas kernels  51.7 us (98%)
  local copies, waits for them, and re-layouts  0.63 us (1%)
    pallas_call x1, Pallas kernels, on_device(): pl.pallas_call(kernel, out_shape=pltpu.VMEM((N, CB), BF), in_specs=[hbm]...  51.7 us

profile of v3, /device:TPU:6, one launch (start us, length us, event | category | flops | bytes accessed | tf_op | source)
XLA Modules:
  0.0 52.4 jit_solution(13424200944948099498)
XLA Ops:
  0.0 51.7 %shard_map.64 = bf16[256,128]{1,0:T(8,128)(2,1)S(1)} custom-call(bf16[256,1024]{1,0:T(8,128)(2,1)} %feat_ref.1, bf16[1024,1024]{1,0:T(8,128)(2,1)} %bitcast.7, f32[1,1024]{1,0:T(1,128)} %asrc_hbm.1, f32[1,1024]{1,0:T(1,128)} %adst_hbm.1, s32[16,64]{1,0:T(8,128)} %bitcast.8, s32[16,64]{1,0:T(8,128)} %bitcast.9), custom_call_target="tpu_custom_call" | custom-call | tf_op jit(solution)/shard_map/pallas_call | solution.py:422
  51.7 0.6 %copy.8 = bf16[256,128]{1,0:T(8,128)(2,1)} copy(bf16[256,128]{1,0:T(8,128)(2,1)S(1)} %shard_map.64) | data formatting | bytes 131072

commit v4 on v3

--- a/solution.py
+++ b/solution.py
@@ -177,13 +177,15 @@
         give(3, j, g, partner)
 
     def stage_near(j):
-        got(0, j, g_l)
         if j in TO_RIGHT:
+            got(0, j, g_l)
             give(2, j, g_l, g_r)
+            got(1, j, g_r)
+        else:
+            got(1, j, g_r)
+            give(2, j, g_r, g_l)
+            got(0, j, g_l)
         give(4, j, g_l, partner)
-        got(1, j, g_r)
-        if j not in TO_RIGHT:
-            give(2, j, g_r, g_l)
         give(5, j, g_r, partner)
 
     def stage_far(j):
@@ -248,7 +250,6 @@
 
     def softmax():
         arrived(s2, r2, m_ss, m_rs, z, in_z)
-        row = lax.broadcasted_iota(jnp.int32, (8, 128), 0)
         lane = lax.broadcasted_iota(jnp.int32, (64, 128), 1)
         neg = -jnp.inf
 
@@ -268,6 +269,10 @@
             return carry
 
         lax.fori_loop(0, 4, max_body, 0)
+
+    def softmax_rest():
+        row = lax.broadcasted_iota(jnp.int32, (8, 128), 0)
+        neg = -jnp.inf
         peak_src = max_cols[...].T[0:8]
         row_n = lax.broadcasted_iota(jnp.int32, (8, N), 0)
         dst_up = pltpu.roll(score, 4, 0)
@@ -303,16 +308,18 @@
     score, iota_n = scores()
     rows_to_group()
     stage_own(1)
+    y_send(3)
     stage_own(7)
-    y_send(3,5)
+    y_send(5)
     scores_along_z()
     stage_near(0)
     stage_own(2)
     stage_own(6)
     y_send(4)
     stage_near(1)
+    softmax()
     stage_near(7)
-    softmax()
+    softmax_rest()
     stage_own(3)
     stage_own(5)
     stage_near(2)
@@ -329,8 +336,8 @@
     stage_near(5)
     stage_far(2)
     stage_pick(1)
+    coefficients()
     stage_pick(7)
-    coefficients()
     stage_near(4)
     stage_far(6)
     stage_pick(2)
@@ -374,6 +381,8 @@
         c.start()
         sent.append(c)
 
+    before = tuple(sent)
+    sent.clear()
     for way, sign in ((0, 1), (1, -1)):
         zs[way, 0] = part(hop(z, 3 * sign, ZN)).astype(BF)
         ring_send(way, 0)
@@ -387,6 +396,8 @@
         zs[way, 2] = part(hop(z, sign, ZN)).astype(BF)
         ring_send(way, 3)
     mine = [part(hop(z, 2 * sign, ZN)) for sign in (1, -1)]
+    for c in before:
+        c.wait_send()
     for way in (0, 1):
         ring(way, 0).wait_recv()
         rows = slice(half * (1 - way), half * (2 - way))

time: 52.8 us -> 52.6 us (level)
  no operation moved by 1% of the time
where the time goes in v4:
time: 52.6 us; the launch traced here: 52.2 us
  Pallas kernels  51.5 us (98%)
  local copies, waits for them, and re-layouts  0.63 us (1%)
    pallas_call x1, Pallas kernels, on_device(): pl.pallas_call(kernel, out_shape=pltpu.VMEM((N, CB), BF), in_specs=[hbm]...  51.5 us

profile of v4, /device:TPU:6, one launch (start us, length us, event | category | flops | bytes accessed | tf_op | source)
XLA Modules:
  0.0 52.2 jit_solution(4948293804345485859)
XLA Ops:
  0.0 51.5 %shard_map.64 = bf16[256,128]{1,0:T(8,128)(2,1)S(1)} custom-call(bf16[256,1024]{1,0:T(8,128)(2,1)} %feat_ref.1, bf16[1024,1024]{1,0:T(8,128)(2,1)} %bitcast.7, f32[1,1024]{1,0:T(1,128)} %asrc_hbm.1, f32[1,1024]{1,0:T(1,128)} %adst_hbm.1, s32[16,64]{1,0:T(8,128)} %bitcast.8, s32[16,64]{1,0:T(8,128)} %bitcast.9), custom_call_target="tpu_custom_call" | custom-call | tf_op jit(solution)/shard_map/pallas_call | solution.py:433
  51.5 0.6 %copy.8 = bf16[256,128]{1,0:T(8,128)(2,1)} copy(bf16[256,128]{1,0:T(8,128)(2,1)S(1)} %shard_map.64) | data formatting | bytes 131072

commit v5 on v4

--- a/solution.py
+++ b/solution.py
@@ -174,7 +174,6 @@
             copy(proj.at[0], pall.at[g, j], y_ss.at[j], y_rs.at[j], in_rel(hop(r, j, RN))).wait_recv()
         give(0, j, g, g_r)
         give(1, j, g, g_l)
-        give(3, j, g, partner)
 
     def stage_near(j):
         if j in TO_RIGHT:
@@ -185,6 +184,7 @@
             got(1, j, g_r)
             give(2, j, g_r, g_l)
             got(0, j, g_l)
+        give(3, j, g, partner)
         give(4, j, g_l, partner)
         give(5, j, g_r, partner)
 

time: 52.6 us -> 52.6 us (level)
  no operation moved by 1% of the time
where the time goes in v5:
time: 52.6 us; the launch traced here: 52.2 us
  Pallas kernels  51.5 us (98%)
  local copies, waits for them, and re-layouts  0.63 us (1%)
    pallas_call x1, Pallas kernels, on_device(): pl.pallas_call(kernel, out_shape=pltpu.VMEM((N, CB), BF), in_specs=[hbm]...  51.5 us

profile of v5, /device:TPU:6, one launch (start us, length us, event | category | flops | bytes accessed | tf_op | source)
XLA Modules:
  0.0 52.2 jit_solution(14217946550484384036)
XLA Ops:
  0.0 51.5 %shard_map.64 = bf16[256,128]{1,0:T(8,128)(2,1)S(1)} custom-call(bf16[256,1024]{1,0:T(8,128)(2,1)} %feat_ref.1, bf16[1024,1024]{1,0:T(8,128)(2,1)} %bitcast.7, f32[1,1024]{1,0:T(1,128)} %asrc_hbm.1, f32[1,1024]{1,0:T(1,128)} %adst_hbm.1, s32[16,64]{1,0:T(8,128)} %bitcast.8, s32[16,64]{1,0:T(8,128)} %bitcast.9), custom_call_target="tpu_custom_call" | custom-call | tf_op jit(solution)/shard_map/pallas_call | solution.py:433
  51.5 0.6 %copy.8 = bf16[256,128]{1,0:T(8,128)(2,1)} copy(bf16[256,128]{1,0:T(8,128)(2,1)S(1)} %shard_map.64) | data formatting | bytes 131072
